TPU v7x, 512 devices: a whole 4x8x8 slice. The times are simulated.
512 devices in a mesh: grp: 16 (over y, core), shard: 32 (over x, z).
Axes of the slice: x: 4, y: 8, z: 8, core: 2. Of those that a mesh axis runs over, the one named last changes fastest.
Arguments:
- table: float32 [32768, 64], P('shard'), may hold values from -6 to 6
- accum: float32 [32768, 64], P('shard'), may hold values from 0.1 to 10
- grad_values: float32 [65536, 64], P(('grp', 'shard')), may hold values from -6 to 6
- grad_rows: int32 [65536], P(('grp', 'shard')), may hold values from 0 to 1023
- grad_counts: int32 [16384], P(('grp', 'shard')), may hold values from 1 to 4
- bucket_ids: int32 [131072, 24, 2], P(('grp', 'shard')), may hold values from 0 to 32767, as said below
- bag_lengths: int32 [131072, 24], P(('grp', 'shard')), may hold values from 1 to 2
- w_hidden: bfloat16 [1536, 1024], P('shard'), may hold values from -0.15625 to 0.15625
- b_hidden: float32 [1024], replicated, may hold values from -3 to 3
- w_score: bfloat16 [1024], replicated, may hold values from -0.1875 to 0.1875
Outputs:
- table_out: float32 [32768, 64], P('shard')
- accum_out: float32 [32768, 64], P('shard')
- scores: float32 [131072], P(('grp', 'shard'))
Inputs may be any that keep to these rules, and one draw needn't show every extreme that they name: `bucket_ids`: counting all 24 x 2 id slots of a device's 256 requests, also those past a bag's length, and calling id // 1024 the owner: one owner gets exactly 768 of them, the same owner for every device of one group along grp, and every other owner's count differs from the others' by at most one.
All inputs are finite; a program needn't handle non-finite values.
Results may differ from a plain program's by a relative error of at most 0.0054.
Values may be sent and summed in bfloat16 or wider, within the bound.
No kernel may reach another device: no remote copies, remote signals or barrier semaphores. Data moves between devices by JAX's collectives and lax.ppermute only.
A program may use at most 64 MiB of HBM per device.

v0:
```python
import math
import jax
import jax.numpy as jnp
from jax import lax
from jax.sharding import PartitionSpec as P


def sum_into_rows(row_count, target_rows, slot_values):
    picks = (jnp.arange(row_count, dtype=jnp.int32)[:, None] == target_rows[None, :]).astype(
        jnp.float32
    )
    return jnp.dot(
        picks, slot_values, precision=lax.Precision.HIGHEST, preferred_element_type=jnp.float32
    )


def build_requests(owner_pick, within, local_rows, capacity):
    owner_total = owner_pick.shape[1]
    within_pick = (within[:, None] == jnp.arange(capacity, dtype=jnp.int32)[None, :]).astype(
        jnp.bfloat16
    )
    low_part = (local_rows % 256).astype(jnp.float32)
    high_part = (local_rows // 256).astype(jnp.float32)
    left_side = jnp.concatenate(
        [owner_pick * low_part[:, None], owner_pick * high_part[:, None]], axis=1
    ).astype(jnp.bfloat16)
    packed = jnp.einsum("sk,sc->kc", left_side, within_pick, preferred_element_type=jnp.float32)
    return (packed[owner_total:] * 256.0 + packed[:owner_total]).astype(jnp.int32)


def per_device(
    table,
    accum,
    grad_values,
    grad_rows,
    grad_counts,
    bucket_ids,
    bag_lengths,
    w_hidden,
    b_hidden,
    w_score,
):
    shard_count = lax.axis_size("shard")
    rows_here, row_width = table.shape
    slot_rows = grad_rows.shape[0] // shard_count
    live_rows = jnp.arange(slot_rows, dtype=jnp.int32)[None, :] < grad_counts[:, None]
    grad_slots = jnp.where(
        live_rows[:, :, None], grad_values.reshape(shard_count, slot_rows, row_width), 0.0
    )
    targets = grad_rows.reshape(shard_count, slot_rows)
    got_values, got_rows = (
        lax.all_to_all(grad_slots, "shard", split_axis=0, concat_axis=0, tiled=True),
        lax.all_to_all(targets, "shard", split_axis=0, concat_axis=0, tiled=True),
    )
    owned_sum = sum_into_rows(rows_here, got_rows.reshape(-1), got_values.reshape(-1, row_width))
    grad_sum = lax.psum(owned_sum, "grp")
    accum_out = accum + grad_sum * grad_sum
    table_out = table - 0.5 * grad_sum * lax.rsqrt(accum_out)
    serving_rows = table_out.astype(jnp.bfloat16)
    request_count, vocab_count, bag_size = bucket_ids.shape
    flat_ids = bucket_ids.reshape(-1)
    slot_count = flat_ids.shape[0]
    capacity = 2 * slot_count // shard_count
    owners = flat_ids // rows_here
    local_rows = flat_ids % rows_here
    owner_iota = jnp.arange(shard_count, dtype=jnp.int32)
    block_len = math.gcd(slot_count, 256)
    block_total = slot_count // block_len
    owner_hot = (
        owners.reshape(block_total, block_len)[:, :, None] == owner_iota[None, None, :]
    ).astype(jnp.bfloat16)
    position = jnp.arange(block_len, dtype=jnp.int32)
    lower_ones = (position[:, None] >= position[None, :]).astype(jnp.bfloat16)
    inclusive = jnp.einsum("ij,bjk->bik", lower_ones, owner_hot, preferred_element_type=jnp.float32)
    owner_float = owner_hot.astype(jnp.float32)
    block_sums = jnp.sum(owner_float, axis=1)
    block_offsets = jnp.cumsum(block_sums, axis=0) - block_sums
    ranks = inclusive + block_offsets[:, None, :]
    within = (jnp.sum(owner_float * ranks, axis=2) - 1.0).reshape(-1).astype(jnp.int32)
    owner_pick = owner_float.reshape(slot_count, shard_count)
    placed = owners * capacity + within
    requested = build_requests(owner_pick, within, local_rows, capacity)
    fetched = serving_rows[
        lax.all_to_all(requested, "shard", split_axis=0, concat_axis=0, tiled=True)
    ]
    returned = lax.all_to_all(fetched, "shard", split_axis=0, concat_axis=0, tiled=True)
    own_rows = returned.reshape(shard_count * capacity, row_width)[placed]
    own_rows = own_rows.reshape(request_count, vocab_count, bag_size, row_width)
    in_bag = jnp.arange(bag_size, dtype=jnp.int32)[None, None, :] < bag_lengths[:, :, None]
    pooled = jnp.sum(jnp.where(in_bag[..., None], own_rows.astype(jnp.float32), 0.0), axis=2)
    pooled = pooled.astype(jnp.bfloat16).reshape(request_count, vocab_count * row_width)
    hidden_pre = jnp.dot(
        pooled,
        lax.all_gather(w_hidden, "shard", axis=0, tiled=True),
        preferred_element_type=jnp.float32,
    )
    hidden = jax.nn.silu(hidden_pre + b_hidden).astype(jnp.bfloat16)
    scores = jnp.dot(hidden, w_score, preferred_element_type=jnp.float32)
    return (table_out, accum_out, scores)


def solution(mesh):
    return jax.shard_map(
        per_device,
        mesh=mesh,
        in_specs=(
            P("shard", None),
            P("shard", None),
            P(("grp", "shard"), None),
            P(("grp", "shard")),
            P(("grp", "shard")),
            P(("grp", "shard"), None, None),
            P(("grp", "shard"), None),
            P("shard", None),
            P(),
            P(),
        ),
        out_specs=(P("shard", None), P("shard", None), P(("grp", "shard"))),
        check_vma=False,
    )
```

profile of v0, /device:TPU:6, one launch (start us, length us, event | category | flops | bytes accessed | tf_op | source)
XLA Modules:
  0.0 444.5 jit_solution(10169167343859944870)
XLA Ops:
  8.0 1.4 all_to_all.20
  9.4 13.4 %all-to-all-start = ((s32[32,1,4]{2,1,0:T(1,128)}), s32[32,1,4]{2,1,0:T(1,128)S(1)}, u32[]{:S(2)}, u32[]{:S(2)}) async-start(s32[32,1,4]{2,1,0:T(1,128)} %bitcast), calls=%async_computation | async-start | bytes 32768 | tf_op jit(solution)/shard_map/all_to_all | solution.py:53
  22.8 1.8 copy.46
  24.7 2.1 reshape.301
  26.8 2.1 reshape.302
  31.2 7.7 %fusion = f32[64,768]{1,0:T(8,128)S(1)} fusion(s32[12288]{0:T(1024)S(1)} %bitcast.41, bf16[12288,32]{0,1:T(8,128)(2,1)S(1)} %get-tuple-element.9, bf16[12288,32]{0,1:T(8,128)(2,1)S(1)} %get-tuple-element.8), kind=kOutput, calls=%fused_computation.3 | convolution fusion | flops 1220542464 | bytes 1818624 | tf_op jit(solution)/shard_map/sk,sc->kc/dot_general | solution.py:27
  39.7 9.8 %all-to-all-start.1 = ((f32[32,1,256]{2,1,0:T(1,128)}), f32[32,1,256]{2,1,0:T(1,128)S(1)}, u32[]{:S(2)}, u32[]{:S(2)}) async-start(f32[32,1,256]{2,1,0:T(1,128)} %reshape.335), calls=%async_computation.1 | async-start | bytes 65536 | tf_op jit(solution)/shard_map/all_to_all | solution.py:52
  51.6 6.0 %all-to-all-done.1 = f32[32,1,256]{2,1,0:T(1,128)S(1)} async-done(((f32[32,1,256]{2,1,0:T(1,128)}), f32[32,1,256]{2,1,0:T(1,128)S(1)}, u32[]{:S(2)}, u32[]{:S(2)}) %all-to-all-start.1) | async-done | bytes 32800 | tf_op jit(solution)/shard_map/all_to_all | solution.py:52
  57.5 5.7 %all-to-all-start.2 = ((s32[32,1,768]{2,1,0:T(1,128)}), s32[32,1,768]{2,1,0:T(1,128)S(1)}, u32[]{:S(2)}, u32[]{:S(2)}) async-start(s32[32,1,768]{2,1,0:T(1,128)} %copy.48), calls=%async_computation.2 | async-start | bytes 196608 | tf_op jit(solution)/shard_map/all_to_all | solution.py:84
  64.7 1.1 fusion.16
  65.8 5.8 %all-to-all-done.2 = s32[32,1,768]{2,1,0:T(1,128)S(1)} async-done(((s32[32,1,768]{2,1,0:T(1,128)}), s32[32,1,768]{2,1,0:T(1,128)S(1)}, u32[]{:S(2)}, u32[]{:S(2)}) %all-to-all-start.2) | async-done | bytes 98336 | tf_op jit(solution)/shard_map/all_to_all | solution.py:84
  72.3 109.3 %all-reduce.2.cloned.1.call-done = f32[1024,64]{0,1:T(8,128)} async-done(((f32[1024,64]{0,1:T(8,128)}), f32[1024,64]{0,1:T(8,128)}) %all-reduce.2.cloned.1.call-update) | async-done | bytes 262160 | tf_op jit(solution)/shard_map/psum | solution.py:56
  181.7 2.0 fusion.32
  183.8 93.6 %gather_fusion = bf16[24576,64]{1,0:T(8,128)(2,1)} fusion(bf16[1024,64]{1,0:T(8,128)(2,1)S(1)} %copy.49, s32[24576]{0:T(1024)} %broadcast_clamp_fusion), kind=kCustom, calls=%fused_computation | custom fusion | bytes 6389760 | tf_op jit(solution)/shard_map/gather | solution.py:83
  277.4 6.8 %copy.50 = bf16[32,768,64]{1,2,0:T(8,128)(2,1)} copy(bf16[32,768,64]{2,1,0:T(8,128)(2,1)} %bitcast.33) | data formatting | bytes 6291456 | tf_op jit(solution)/shard_map/gather | solution.py:83
  284.3 10.6 %all-to-all-start.3 = ((bf16[32,768,64]{1,2,0:T(8,128)(2,1)}), bf16[32,768,64]{1,2,0:T(8,128)(2,1)}, u32[]{:S(2)}, u32[]{:S(2)}) async-start(bf16[32,768,64]{1,2,0:T(8,128)(2,1)} %copy.50), calls=%async_computation.3 | async-start | bytes 6291456 | tf_op jit(solution)/shard_map/all_to_all | solution.py:86
  295.5 2.2 reshape.304
  297.9 2.2 iota_compare_fusion.2
  300.4 72.3 %all-to-all-done.3 = bf16[32,768,64]{1,2,0:T(8,128)(2,1)} async-done(((bf16[32,768,64]{1,2,0:T(8,128)(2,1)}), bf16[32,768,64]{1,2,0:T(8,128)(2,1)}, u32[]{:S(2)}, u32[]{:S(2)}) %all-to-all-start.3) | async-done | bytes 3145760 | tf_op jit(solution)/shard_map/all_to_all | solution.py:86
  372.7 6.6 %copy.51 = bf16[32,768,64]{2,1,0:T(8,128)(2,1)} copy(bf16[32,768,64]{1,2,0:T(8,128)(2,1)} %all-to-all-done.3) | data formatting | bytes 6291456 | tf_op jit(solution)/shard_map/all_to_all | solution.py:86
  379.3 36.4 %gather_fusion.1 = bf16[12288,64]{1,0:T(8,128)(2,1)S(1)} fusion(bf16[24576,64]{1,0:T(8,128)(2,1)} %bitcast.32, s32[12288]{0:T(1024)S(1)} %broadcast_clamp_fusion.1), kind=kCustom, calls=%fused_computation.1 | custom fusion | bytes 3194880 | tf_op jit(solution)/shard_map/gather | solution.py:87
  415.8 15.5 %fusion.2 = bf16[256,24,64]{2,1,0:T(8,128)(2,1)} fusion(bf16[256,24,2,64]{3,2,1,0:T(2,128)(2,1)S(1)} %bitcast.34, pred[256,24,2]{2,1,0:T(8,128)(4,1)} %iota_compare_fusion.2), kind=kLoop, calls=%fused_computation.6 | loop fusion | flops 1966080 | bytes 2371584 | tf_op jit(solution)/shard_map/reduce_sum | solution.py:90
  431.3 2.0 copy.53
  433.3 3.7 fusion.12
  (47 shorter events, 8.5 us)
Async XLA Ops:
  9.4 30.3 %all-to-all-start = ((s32[32,1,4]{2,1,0:T(1,128)}), s32[32,1,4]{2,1,0:T(1,128)S(1)}, u32[]{:S(2)}, u32[]{:S(2)}) async-start(s32[32,1,4]{2,1,0:T(1,128)} %bitcast), calls=%async_computation | async-start | bytes 32768 | tf_op jit(solution)/shard_map/all_to_all | solution.py:53
  26.8 4.0 copy-start.1
  26.8 4.1 copy-start.4
  39.7 17.8 %all-to-all-start.1 = ((f32[32,1,256]{2,1,0:T(1,128)}), f32[32,1,256]{2,1,0:T(1,128)S(1)}, u32[]{:S(2)}, u32[]{:S(2)}) async-start(f32[32,1,256]{2,1,0:T(1,128)} %reshape.335), calls=%async_computation.1 | async-start | bytes 65536 | tf_op jit(solution)/shard_map/all_to_all | solution.py:52
  57.5 14.1 %all-to-all-start.2 = ((s32[32,1,768]{2,1,0:T(1,128)}), s32[32,1,768]{2,1,0:T(1,128)S(1)}, u32[]{:S(2)}, u32[]{:S(2)}) async-start(s32[32,1,768]{2,1,0:T(1,128)} %copy.48), calls=%async_computation.2 | async-start | bytes 196608 | tf_op jit(solution)/shard_map/all_to_all | solution.py:84
  63.3 118.4 %all-reduce.2.cloned.1.call-start = ((), (), s32[]{:S(2)}) async-start(), calls=%async_computation.4 | async-start | bytes 524288 | tf_op jit(solution)/shard_map/psum | solution.py:56
  284.3 88.4 %all-to-all-start.3 = ((bf16[32,768,64]{1,2,0:T(8,128)(2,1)}), bf16[32,768,64]{1,2,0:T(8,128)(2,1)}, u32[]{:S(2)}, u32[]{:S(2)}) async-start(bf16[32,768,64]{1,2,0:T(8,128)(2,1)} %copy.50), calls=%async_computation.3 | async-start | bytes 6291456 | tf_op jit(solution)/shard_map/all_to_all | solution.py:86
  294.9 2.8 copy-start
  294.9 2.9 copy-start.2
  294.9 3.0 copy-start.3
  294.9 138.4 %all-gather.2.cloned.1.call-start = ((), (), s32[]{:S(2)}) async-start(), calls=%async_computation.5 | async-start | bytes 3244032 | tf_op jit(solution)/shard_map/all_gather | solution.py:94
  415.8 17.6 %copy-start.5 = (f32[1024]{0:T(1024)S(1)}, f32[1024]{0:T(1024)}, u32[]{:S(2)}) copy-start(f32[1024]{0:T(1024)} %param.18) | copy-start | bytes 12292
Sparse Core Ops, SparseCore 0:
  67.0 114.6 all-reduce.1
Sparse Core Ops, SparseCore 1:
  299.0 94.9 all-gather.1
where the time goes:
time: 447 us; the launch traced here: 445 us
  waiting for transfers between devices  194 us (43%)
  local copies, waits for them, and re-layouts  158 us (35%)
  starting transfers between devices  39.6 us (9%)
  other arithmetic  23.7 us (5%)
  between operations  15.8 us (4%)
  matrix products  13.2 us (3%)
    psum x1, waiting for transfers between devices, per_device(): grad_sum = lax.psum(owned_sum, 'grp')  109 us
    gather x2, local copies, waits for them, and re-layouts, per_device(): serving_rows[lax.all_to_all(requested, 'shard', split_axis=0, concat_axis...  100 us
    all_to_all x1, waiting for transfers between devices, per_device(): lax.all_to_all(fetched, 'shard', split_axis=0, concat_axis=0, tiled=True)  72.3 us
    gather x1, local copies, waits for them, and re-layouts, per_device(): own_rows = returned.reshape(shard_count * capacity, row_width)[placed]  36.4 us
    reduce_sum x1, other arithmetic, per_device(): jnp.sum(jnp.where(in_bag[..., None], own_rows.astype(jnp.float32), 0.0),...  15.5 us
    all_to_all x1, starting transfers between devices, per_device(): lax.all_to_all(targets, 'shard', split_axis=0, concat_axis=0, tiled=True)  13.4 us
    all_to_all x1, starting transfers between devices, per_device(): lax.all_to_all(fetched, 'shard', split_axis=0, concat_axis=0, tiled=True)  10.6 us
    all_to_all x1, starting transfers between devices, per_device(): lax.all_to_all(grad_slots, 'shard', split_axis=0, concat_axis=0, tiled=True)  9.78 us
  transfers between devices with their start and end apart: 6, of which 4 were waited for; matrix products, arithmetic and copies ran while one was open for 20% of the time, Pallas kernels for 0%

commit v1 on v0

--- a/solution.py
+++ b/solution.py
@@ -53,7 +53,9 @@
         lax.all_to_all(targets, "shard", split_axis=0, concat_axis=0, tiled=True),
     )
     owned_sum = sum_into_rows(rows_here, got_rows.reshape(-1), got_values.reshape(-1, row_width))
-    grad_sum = lax.psum(owned_sum, "grp")
+    grad_sum = owned_sum
+    for hop in (1, 2, 4, 8):
+        grad_sum = grad_sum + lax.ppermute(grad_sum, "grp", [(dev, dev ^ hop) for dev in range(16)])
     accum_out = accum + grad_sum * grad_sum
     table_out = table - 0.5 * grad_sum * lax.rsqrt(accum_out)
     serving_rows = table_out.astype(jnp.bfloat16)

time: 447 us -> 375 us (0.84)
  waiting for transfers between devices: 194 us -> 102 us
  starting transfers between devices: 39.6 us -> 56.2 us
    psum x1 -> x0, waiting for transfers between devices: 109 us -> none  [per_device(): grad_sum = lax.psum(owned_sum, 'grp')]
    ppermute x0 -> x4, waiting for transfers between devices: none -> 22.3 us  [per_device(): lax.ppermute(grad_sum, 'grp', [(dev, dev ^ hop) for dev in range(16)])]
    ppermute x0 -> x4, starting transfers between devices: none -> 17.8 us  [per_device(): lax.ppermute(grad_sum, 'grp', [(dev, dev ^ hop) for dev in range(16)])]
  transfers between devices with their start and end apart: 6 -> 9, of which waited for: 4 -> 6; matrix products, arithmetic and copies ran while one was open for 20% -> 24% of each run, Pallas kernels for 0% -> 0%
where the time goes in v1:
time: 375 us; the launch traced here: 373 us
  local copies, waits for them, and re-layouts  158 us (42%)
  waiting for transfers between devices  102 us (27%)
  starting transfers between devices  56.2 us (15%)
  other arithmetic  27.5 us (7%)
  between operations  14.4 us (4%)
  matrix products  13.7 us (4%)
    gather x2, local copies, waits for them, and re-layouts, per_device(): serving_rows[lax.all_to_all(requested, 'shard', split_axis=0, concat_axis...  101 us
    all_to_all x1, waiting for transfers between devices, per_device(): lax.all_to_all(fetched, 'shard', split_axis=0, concat_axis=0, tiled=True)  71.9 us
    gather x1, local copies, waits for them, and re-layouts, per_device(): own_rows = returned.reshape(shard_count * capacity, row_width)[placed]  36.4 us
    ppermute x4, waiting for transfers between devices, per_device(): lax.ppermute(grad_sum, 'grp', [(dev, dev ^ hop) for dev in range(16)])  22.3 us
    ppermute x4, starting transfers between devices, per_device(): lax.ppermute(grad_sum, 'grp', [(dev, dev ^ hop) for dev in range(16)])  17.8 us
    reduce_sum x1, other arithmetic, per_device(): jnp.sum(jnp.where(in_bag[..., None], own_rows.astype(jnp.float32), 0.0),...  15.5 us
    all_to_all x1, starting transfers between devices, per_device(): lax.all_to_all(targets, 'shard', split_axis=0, concat_axis=0, tiled=True)  13.5 us
    all_to_all x1, starting transfers between devices, per_device(): lax.all_to_all(grad_slots, 'shard', split_axis=0, concat_axis=0, tiled=True)  9.78 us
  transfers between devices with their start and end apart: 9, of which 6 were waited for; matrix products, arithmetic and copies ran while one was open for 24% of the time, Pallas kernels for 0%

profile of v1, /device:TPU:6, one launch (start us, length us, event | category | flops | bytes accessed | tf_op | source)
XLA Modules:
  0.0 372.6 jit_solution(5045257643165559417)
XLA Ops:
  8.5 13.5 %all-to-all-start = ((s32[32,1,4]{2,1,0:T(1,128)}), s32[32,1,4]{2,1,0:T(1,128)S(1)}, u32[]{:S(2)}, u32[]{:S(2)}) async-start(s32[32,1,4]{2,1,0:T(1,128)} %bitcast), calls=%async_computation | async-start | bytes 32768 | tf_op jit(solution)/shard_map/all_to_all | solution.py:53
  23.9 2.1 reshape.301
  26.0 2.1 reshape.302
  31.7 9.8 %all-to-all-start.1 = ((f32[32,1,256]{2,1,0:T(1,128)}), f32[32,1,256]{2,1,0:T(1,128)S(1)}, u32[]{:S(2)}, u32[]{:S(2)}) async-start(f32[32,1,256]{2,1,0:T(1,128)} %reshape.335), calls=%async_computation.1 | async-start | bytes 65536 | tf_op jit(solution)/shard_map/all_to_all | solution.py:52
  43.5 6.1 %all-to-all-done.1 = f32[32,1,256]{2,1,0:T(1,128)S(1)} async-done(((f32[32,1,256]{2,1,0:T(1,128)}), f32[32,1,256]{2,1,0:T(1,128)S(1)}, u32[]{:S(2)}, u32[]{:S(2)}) %all-to-all-start.1) | async-done | bytes 32800 | tf_op jit(solution)/shard_map/all_to_all | solution.py:52
  51.3 2.1 collective-permute-start
  53.4 8.9 %fusion = f32[64,768]{1,0:T(8,128)S(1)} fusion(s32[12288]{0:T(1024)S(1)} %bitcast.41, bf16[12288,32]{0,1:T(8,128)(2,1)} %get-tuple-element.9, bf16[12288,32]{0,1:T(8,128)(2,1)} %get-tuple-element.8), kind=kOutput, calls=%fused_computation.3 | convolution fusion | flops 1220542464 | bytes 1818624 | tf_op jit(solution)/shard_map/sk,sc->kc/dot_general | solution.py:27
  62.3 3.5 collective-permute-start.1
  66.6 5.7 %all-to-all-start.2 = ((s32[32,1,768]{2,1,0:T(1,128)}), s32[32,1,768]{2,1,0:T(1,128)S(1)}, u32[]{:S(2)}, u32[]{:S(2)}) async-start(s32[32,1,768]{2,1,0:T(1,128)} %copy.48), calls=%async_computation.2 | async-start | bytes 196608 | tf_op jit(solution)/shard_map/all_to_all | solution.py:86
  74.7 4.5 %collective-permute-start.2 = (f32[1024,64]{0,1:T(8,128)}, f32[1024,64]{0,1:T(8,128)S(1)}, u32[]{:S(2)}, u32[]{:S(2)}) collective-permute-start(f32[1024,64]{0,1:T(8,128)} %add.131), channel_id=1, source_target_pairs={{0,128},{32,160},{64,192},{96,224},{128,0},{160,32},{192,64},{224,... | collective-permute-start | bytes 786440 | tf_op jit(solution)/shard_map/ppermute | solution.py:58
  81.0 10.3 %collective-permute-done.2 = f32[1024,64]{0,1:T(8,128)S(1)} collective-permute-done((f32[1024,64]{0,1:T(8,128)}, f32[1024,64]{0,1:T(8,128)S(1)}, u32[]{:S(2)}, u32[]{:S(2)}) %collective-permute-start.2) | collective-permute-done | bytes 262176 | tf_op jit(solution)/shard_map/ppermute | solution.py:58
  92.2 7.7 %collective-permute-start.3 = (f32[1024,64]{0,1:T(8,128)S(1)}, f32[1024,64]{0,1:T(8,128)S(1)}, u32[]{:S(2)}, u32[]{:S(2)}) collective-permute-start(f32[1024,64]{0,1:T(8,128)S(1)} %add.132), channel_id=1, source_target_pairs={{0,256},{32,288},{64,320},{96,352},{128,384},{160,416},{192,448},{... | collective-permute-start | bytes 786440 | tf_op jit(solution)/shard_map/ppermute | solution.py:58
  100.6 11.4 %collective-permute-done.3 = f32[1024,64]{0,1:T(8,128)S(1)} collective-permute-done((f32[1024,64]{0,1:T(8,128)S(1)}, f32[1024,64]{0,1:T(8,128)S(1)}, u32[]{:S(2)}, u32[]{:S(2)}) %collective-permute-start.3) | collective-permute-done | bytes 262176 | tf_op jit(solution)/shard_map/ppermute | solution.py:58
  114.1 93.7 %gather_fusion = bf16[24576,64]{1,0:T(8,128)(2,1)} fusion(bf16[1024,64]{1,0:T(8,128)(2,1)S(1)} %copy.49, s32[24576]{0:T(1024)} %broadcast_clamp_fusion), kind=kCustom, calls=%fused_computation | custom fusion | bytes 6389760 | tf_op jit(solution)/shard_map/gather | solution.py:85
  207.7 6.8 %copy.50 = bf16[32,768,64]{1,2,0:T(8,128)(2,1)} copy(bf16[32,768,64]{2,1,0:T(8,128)(2,1)} %bitcast.33) | data formatting | bytes 6291456 | tf_op jit(solution)/shard_map/gather | solution.py:85
  214.6 9.2 %all-to-all-start.3 = ((bf16[32,768,64]{1,2,0:T(8,128)(2,1)}), bf16[32,768,64]{1,2,0:T(8,128)(2,1)}, u32[]{:S(2)}, u32[]{:S(2)}) async-start(bf16[32,768,64]{1,2,0:T(8,128)(2,1)} %copy.50), calls=%async_computation.3 | async-start | bytes 6291456 | tf_op jit(solution)/shard_map/all_to_all | solution.py:88
  224.5 2.2 reshape.304
  226.9 2.2 iota_compare_fusion.2
  229.4 71.9 %all-to-all-done.3 = bf16[32,768,64]{1,2,0:T(8,128)(2,1)} async-done(((bf16[32,768,64]{1,2,0:T(8,128)(2,1)}), bf16[32,768,64]{1,2,0:T(8,128)(2,1)}, u32[]{:S(2)}, u32[]{:S(2)}) %all-to-all-start.3) | async-done | bytes 3145760 | tf_op jit(solution)/shard_map/all_to_all | solution.py:88
  301.3 6.7 %copy.51 = bf16[32,768,64]{2,1,0:T(8,128)(2,1)} copy(bf16[32,768,64]{1,2,0:T(8,128)(2,1)} %all-to-all-done.3) | data formatting | bytes 6291456 | tf_op jit(solution)/shard_map/all_to_all | solution.py:88
  308.0 36.4 %gather_fusion.1 = bf16[12288,64]{1,0:T(8,128)(2,1)S(1)} fusion(bf16[24576,64]{1,0:T(8,128)(2,1)} %bitcast.32, s32[12288]{0:T(1024)S(1)} %broadcast_clamp_fusion.1), kind=kCustom, calls=%fused_computation.1 | custom fusion | bytes 3194880 | tf_op jit(solution)/shard_map/gather | solution.py:89
  344.4 15.5 %fusion.2 = bf16[256,24,64]{2,1,0:T(8,128)(2,1)} fusion(bf16[256,24,2,64]{3,2,1,0:T(2,128)(2,1)S(1)} %bitcast.34, pred[256,24,2]{2,1,0:T(8,128)(4,1)} %iota_compare_fusion.2), kind=kLoop, calls=%fused_computation.6 | loop fusion | flops 1966080 | bytes 2371584 | tf_op jit(solution)/shard_map/reduce_sum | solution.py:92
  360.0 2.0 copy.53
  362.0 3.7 %fusion.12 = f32[1,256]{1,0:T(1,128)} fusion(bf16[1024,1]{0,1:T(2,128)(2,1)S(1)} %reshape.324, bf16[256,1536]{0,1:T(8,128)(2,1)S(1)} %bitcast.35, bf16[1536,1024]{1,0:T(8,128)(2,1)} %all-gather.2.cloned.1.call-done, f32[1024]{0:T(1024)S(1)} %copy-done.5), kind=kOutput, calls=%fused_computation.25 | convolution fusion | flops 807403520 | bytes 3939328 | tf_op jit(solution)/shard_map/dot_general | solution.py:100
  (55 shorter events, 20.3 us)
Async XLA Ops:
  8.5 23.2 %all-to-all-start = ((s32[32,1,4]{2,1,0:T(1,128)}), s32[32,1,4]{2,1,0:T(1,128)S(1)}, u32[]{:S(2)}, u32[]{:S(2)}) async-start(s32[32,1,4]{2,1,0:T(1,128)} %bitcast), calls=%async_computation | async-start | bytes 32768 | tf_op jit(solution)/shard_map/all_to_all | solution.py:53
  23.8 4.8 %copy-start.1 = (f32[128,64]{0,1:T(8,128)S(1)}, f32[128,64]{0,1:T(8,128)}, u32[]{:S(2)}) copy-start(f32[128,64]{0,1:T(8,128)} %param.12) | copy-start | bytes 98308
  23.9 4.8 %copy-start.4 = (s32[32]{0:T(128)S(1)}, s32[32]{0:T(128)}, u32[]{:S(2)}) copy-start(s32[32]{0:T(128)} %param.14) | copy-start | bytes 388
  31.7 17.8 %all-to-all-start.1 = ((f32[32,1,256]{2,1,0:T(1,128)}), f32[32,1,256]{2,1,0:T(1,128)S(1)}, u32[]{:S(2)}, u32[]{:S(2)}) async-start(f32[32,1,256]{2,1,0:T(1,128)} %reshape.335), calls=%async_computation.1 | async-start | bytes 65536 | tf_op jit(solution)/shard_map/all_to_all | solution.py:52
  51.3 11.0 %collective-permute-start = (f32[1024,64]{0,1:T(8,128)S(1)}, f32[1024,64]{0,1:T(8,128)S(1)}, u32[]{:S(2)}, u32[]{:S(2)}) collective-permute-start(f32[1024,64]{0,1:T(8,128)S(1)} %fusion.16), channel_id=1, source_target_pairs={{0,32},{32,0},{64,96},{96,64},{128,160},{160,128},{192,224},{224,1... | collective-permute-start | bytes 786440 | tf_op jit(solution)/shard_map/ppermute | solution.py:58
  62.3 10.7 %collective-permute-start.1 = (f32[1024,64]{0,1:T(8,128)S(1)}, f32[1024,64]{0,1:T(8,128)}, u32[]{:S(2)}, u32[]{:S(2)}) collective-permute-start(f32[1024,64]{0,1:T(8,128)S(1)} %add.130), channel_id=1, source_target_pairs={{0,64},{32,96},{64,0},{96,32},{128,192},{160,224},{192,128},{224,1... | collective-permute-start | bytes 786440 | tf_op jit(solution)/shard_map/ppermute | solution.py:58
  66.6 14.3 %all-to-all-start.2 = ((s32[32,1,768]{2,1,0:T(1,128)}), s32[32,1,768]{2,1,0:T(1,128)S(1)}, u32[]{:S(2)}, u32[]{:S(2)}) async-start(s32[32,1,768]{2,1,0:T(1,128)} %copy.48), calls=%async_computation.2 | async-start | bytes 196608 | tf_op jit(solution)/shard_map/all_to_all | solution.py:86
  74.7 16.5 %collective-permute-start.2 = (f32[1024,64]{0,1:T(8,128)}, f32[1024,64]{0,1:T(8,128)S(1)}, u32[]{:S(2)}, u32[]{:S(2)}) collective-permute-start(f32[1024,64]{0,1:T(8,128)} %add.131), channel_id=1, source_target_pairs={{0,128},{32,160},{64,192},{96,224},{128,0},{160,32},{192,64},{224,... | collective-permute-start | bytes 786440 | tf_op jit(solution)/shard_map/ppermute | solution.py:58
  92.2 19.8 %collective-permute-start.3 = (f32[1024,64]{0,1:T(8,128)S(1)}, f32[1024,64]{0,1:T(8,128)S(1)}, u32[]{:S(2)}, u32[]{:S(2)}) collective-permute-start(f32[1024,64]{0,1:T(8,128)S(1)} %add.132), channel_id=1, source_target_pairs={{0,256},{32,288},{64,320},{96,352},{128,384},{160,416},{192,448},{... | collective-permute-start | bytes 786440 | tf_op jit(solution)/shard_map/ppermute | solution.py:58
  214.6 86.8 %all-to-all-start.3 = ((bf16[32,768,64]{1,2,0:T(8,128)(2,1)}), bf16[32,768,64]{1,2,0:T(8,128)(2,1)}, u32[]{:S(2)}, u32[]{:S(2)}) async-start(bf16[32,768,64]{1,2,0:T(8,128)(2,1)} %copy.50), calls=%async_computation.3 | async-start | bytes 6291456 | tf_op jit(solution)/shard_map/all_to_all | solution.py:88
  223.7 3.0 copy-start
  223.8 3.0 copy-start.2
  223.8 3.1 copy-start.3
  223.8 138.2 %all-gather.2.cloned.1.call-start = ((), (), s32[]{:S(2)}) async-start(), calls=%async_computation.4 | async-start | bytes 3244032 | tf_op jit(solution)/shard_map/all_gather | solution.py:96
  344.4 17.6 %copy-start.5 = (f32[1024]{0:T(1024)S(1)}, f32[1024]{0:T(1024)}, u32[]{:S(2)}) copy-start(f32[1024]{0:T(1024)} %param.18) | copy-start | bytes 12292
Sparse Core Ops, SparseCore 0:
  227.8 93.0 all-gather.1
